TPU v7x, 128 devices: a whole 4x4x4 slice. The times are simulated.
128 devices in a mesh: dom: 32 (over y, x, core), grp: 4 (over z).
Axes of the slice: x: 4, y: 4, z: 4, core: 2. Of those that a mesh axis runs over, the one named last changes fastest.
Arguments:
- encoded: float32 [65536, 1024], P(('dom', 'grp')), may hold values from -6 to 6
- owner_of: int32 [65536], P(('dom', 'grp')), may hold values from 0 to 65535, as said below
- nbr_blocks: int32 [512, 16], P(('dom', 'grp')), may hold values from 0 to 15, as said below
- nbr_count: int32 [512], P(('dom', 'grp')), may hold values from 1 to 16, as said below
- edge_weights: bfloat16 [512, 16, 128, 128], P(('dom', 'grp')), may hold values from 0.01 to 16
Outputs:
- propagated: bfloat16 [65536, 1024], P(('dom', 'grp'))
Inputs may be any that keep to these rules, and one draw needn't show every extreme that they name: owner_of is a permutation; the batch rows of each device go to the nodes of every device in equal numbers (512 / the device count to each), where device d owns nodes d * 512 to (d + 1) * 512 - 1. `nbr_blocks`: A partition group is the 2048 nodes of the devices that share a dom index; block g of a group is its nodes g * 128 to (g + 1) * 128 - 1. The first nbr_count[b] entries of row block b are distinct; later entries are padding and are ignored. `nbr_count`: some row block has exactly 16 live blocks.
All inputs are finite; a program needn't handle non-finite values.
Results may differ from a plain program's by a relative error of at most 0.005.
Values may be sent and summed in bfloat16 or wider, within the bound.
No kernel may reach another device: no remote copies, remote signals or barrier semaphores. Data moves between devices by JAX's collectives and lax.ppermute only.
A program may use at most 64 MiB of HBM per device.

v0:
```python
import jax
import jax.numpy as jnp
from jax import lax
from jax.sharding import PartitionSpec as P

STEPS = 2
mix_weight = 0.3


def propagate(base_rows, weight_table, list_table, count_table, panel_blocks, gather_panel):
    block_count, slot_count, block_size, _ = weight_table.shape
    live_table = jnp.arange(slot_count, dtype=jnp.int32)[None, :] < count_table[:, None]
    picks = (
        list_table[:, :, None] == jnp.arange(panel_blocks, dtype=jnp.int32)[None, None, :]
    ) & live_table[:, :, None]
    select = picks.astype(jnp.bfloat16)
    dense = jnp.einsum(
        "bkg,bkpq->bpgq", select, weight_table, preferred_element_type=jnp.float32
    ).astype(jnp.bfloat16)
    dense = dense.reshape(block_count * block_size, panel_blocks * block_size)
    degree = jnp.sum(dense, axis=1, dtype=jnp.float32)
    row_scale = lax.rsqrt(degree)[:, None]
    hidden = base_rows.astype(jnp.bfloat16)
    for step_index in range(STEPS):
        panel_rows = gather_panel(hidden)
        running = jnp.dot(dense, panel_rows, preferred_element_type=jnp.float32)
        hidden = (mix_weight * base_rows + (1.0 - mix_weight) * running * row_scale).astype(
            jnp.bfloat16
        )
    return hidden


def shards(encoded, owner_of, nbr_blocks, nbr_count, edge_weights):
    row_count, feat_width = encoded.shape
    block_count, slot_count, block_size, _ = edge_weights.shape
    target_dev = owner_of // row_count
    send_order = jnp.argsort(target_dev, stable=True)
    row_ids = jnp.arange(row_count, dtype=jnp.int32)
    send_pick = (send_order[:, None] == row_ids[None, :]).astype(jnp.float32)
    outgoing = jnp.dot(
        send_pick, encoded, precision=lax.Precision.HIGHEST, preferred_element_type=jnp.float32
    )
    places = jnp.take(owner_of, send_order, axis=0)
    arrived, where_to = (
        lax.all_to_all(
            outgoing.astype(jnp.bfloat16), ("dom", "grp"), split_axis=0, concat_axis=0, tiled=True
        ).astype(outgoing.dtype),
        lax.all_to_all(places, ("dom", "grp"), split_axis=0, concat_axis=0, tiled=True),
    )
    place_pick = (row_ids[:, None] == (where_to % row_count)[None, :]).astype(jnp.float32)
    base_rows = jnp.dot(
        place_pick, arrived, precision=lax.Precision.HIGHEST, preferred_element_type=jnp.float32
    )

    def group_panel(hidden):
        return lax.all_gather(hidden, "grp", axis=0, tiled=True)

    panel_blocks = block_count * lax.axis_size("grp")
    return propagate(base_rows, edge_weights, nbr_blocks, nbr_count, panel_blocks, group_panel)


def solution(mesh):
    return jax.shard_map(
        shards,
        mesh=mesh,
        in_specs=(
            P(("dom", "grp"), None),
            P(("dom", "grp")),
            P(("dom", "grp"), None),
            P(("dom", "grp")),
            P(("dom", "grp"), None, None, None),
        ),
        out_specs=P(("dom", "grp"), None),
        check_vma=False,
    )
```

profile of v0, /device:TPU:1, one launch (start us, length us, event | category | flops | bytes accessed | tf_op | source)
XLA Modules:
  0.0 179.5 jit_solution(9671089370718514029)
XLA Ops:
  6.5 0.0 copy-start
  6.5 0.8 add_select_fusion.1
  7.4 3.8 %sort.17 = (s32[512]{0:T(512)}, s32[512]{0:T(512)S(1)}) sort(s32[512]{0:T(512)S(1)} %add_select_fusion.1, s32[512]{0:T(512)S(1)} %iota.22), dimensions={0}, to_apply=%region_0.1 | sort | flops 4608 | bytes 8192 | tf_op jit(solution)/shard_map/jit(argsort)/sort | solution.py:37
  11.2 3.6 %gather_fusion = s32[512]{0:T(512)S(1)} fusion(s32[512]{0:T(512)} %param.6, s32[1024]{0:T(1024)S(1)} %pad_clamp_fusion), kind=kCustom, calls=%fused_computation | custom fusion | bytes 6144 | tf_op jit(solution)/shard_map/jit(_take)/gather | solution.py:43
  14.8 0.7 select_n.37
  15.5 11.5 %all-to-all-start = ((s32[128,4,1]{1,2,0:T(1,128)}), s32[128,4,1]{1,2,0:T(1,128)S(1)}, u32[]{:S(2)}, u32[]{:S(2)}) async-start(s32[128,4,1]{1,2,0:T(1,128)} %bitcast), calls=%async_computation | async-start | bytes 131072 | tf_op jit(solution)/shard_map/all_to_all | solution.py:48
  27.0 3.6 %convolution_convert_fusion = bf16[512,1024]{1,0:T(8,128)(2,1)S(1)} fusion(f32[512,1024]{1,0:T(8,128)} %param.5, s32[512]{0:T(512)S(1)} %get-tuple-element.6), kind=kOutput, calls=%fused_computation.13 | convolution fusion | flops 3222011904 | bytes 3147776 | tf_op jit(solution)/shard_map/dot_general | solution.py:40
  30.6 1.2 all_to_all.16
  31.8 4.8 %all-to-all-done = s32[128,4,1]{1,2,0:T(1,128)S(1)} async-done(((s32[128,4,1]{1,2,0:T(1,128)}), s32[128,4,1]{1,2,0:T(1,128)S(1)}, u32[]{:S(2)}, u32[]{:S(2)}) %all-to-all-start) | async-done | bytes 2080 | tf_op jit(solution)/shard_map/all_to_all | solution.py:48
  36.6 5.0 %all-to-all-start.1 = ((bf16[128,4,1024]{2,1,0:T(4,128)(2,1)}), bf16[128,4,1024]{2,1,0:T(4,128)(2,1)S(1)}, u32[]{:S(2)}, u32[]{:S(2)}) async-start(bf16[128,4,1024]{2,1,0:T(4,128)(2,1)} %all_to_all.16), calls=%async_computation.1 | async-start | bytes 2097152 | tf_op jit(solution)/shard_map/all_to_all | solution.py:45
  41.6 0.0 all-gather.3.cloned.1.call-start
  41.6 0.5 broadcast.84
  42.2 0.8 reduce.4
  43.0 0.1 all_to_all.15
  43.1 17.9 %all-to-all-done.1 = bf16[128,4,1024]{2,1,0:T(4,128)(2,1)S(1)} async-done(((bf16[128,4,1024]{2,1,0:T(4,128)(2,1)}), bf16[128,4,1024]{2,1,0:T(4,128)(2,1)S(1)}, u32[]{:S(2)}, u32[]{:S(2)}) %all-to-all-start.1) | async-done | bytes 1048608 | tf_op jit(solution)/shard_map/all_to_all | solution.py:45
  61.0 1.1 all_to_all.18
  62.1 0.0 copy-start.2
  62.1 0.0 copy-start.1
  62.1 3.7 %fusion.26 = (bf16[512,1024]{1,0:T(8,128)(2,1)}, f32[512,1024]{1,0:T(8,128)}) fusion(bf16[512,1024]{1,0:T(8,128)(2,1)} %all_to_all.18, s32[512]{0:T(512)S(1)} %add_select_fusion), kind=kOutput, calls=%fused_computation.40 | convolution fusion | flops 537657344 | bytes 4196352 | tf_op jit(solution)/shard_map/dot_general | solution.py:51
  65.8 0.0 all-gather.3.cloned.1.call-update
  65.8 0.2 all-gather.5.cloned.1.call-start
  66.1 0.0 copy-done.2
  66.1 0.1 iota_compare_fusion.5
  66.1 0.0 copy-done
  66.1 0.0 copy-done.1
  66.1 3.6 %convert_reduce_fusion = (f32[4,128]{1,0:T(4,128)S(1)}, bf16[4,16,128,128]{3,1,2,0:T(8,128)(2,1)}) fusion(bf16[4,16,128,128]{3,2,1,0:T(8,128)(2,1)S(1)} %copy-done, s32[4,16]{1,0:T(4,128)S(1)} %copy-done.1, pred[4,16]{1,0:T(4,128)(4,1)S(1)} %iota_compare_fusion.5), kind=kOutput, calls=%fused_computation.1 | convolution fusion | flops 36701696 | bytes 4196672 | tf_op jit(solution)/shard_map/bkg,bkpq->bpgq/dot_general | solution.py:17
  69.8 40.5 %all-gather.3.cloned.1.call-done = bf16[2048,1024]{1,0:T(8,128)(2,1)} async-done(((bf16[512,1024]{1,0:T(8,128)(2,1)}), bf16[2048,1024]{1,0:T(8,128)(2,1)}) %all-gather.3.cloned.1.call-update) | async-done | bytes 4194320 | tf_op jit(solution)/shard_map/all_gather | solution.py:56
  110.2 6.8 %add_convert_fusion.1 = bf16[512,1024]{1,0:T(8,128)(2,1)} fusion(f32[512,1024]{1,0:T(8,128)} %get-tuple-element.8, bf16[2048,1024]{1,0:T(8,128)(2,1)} %all-gather.3.cloned.1.call-done, bf16[64,8,16,128]{3,2,1,0:T(8,128)(2,1)} %bitcast.28, f32[512]{0:T(512)S(1)} %multiply_bitcast_fusion), kind=kOutput, calls=%fused_computation.9 | convolution fusion | flops 2149580800 | bytes 9439232 | tf_op jit(solution)/shard_map/dot_general | solution.py:26
  117.0 0.0 all-gather.5.cloned.1.call-update
  117.0 48.8 %all-gather.5.cloned.1.call-done = bf16[2048,1024]{1,0:T(8,128)(2,1)} async-done(((bf16[512,1024]{1,0:T(8,128)(2,1)}), bf16[2048,1024]{1,0:T(8,128)(2,1)}) %all-gather.5.cloned.1.call-update) | async-done | bytes 4194320 | tf_op jit(solution)/shard_map/all_gather | solution.py:56
  165.9 6.8 %add_convert_fusion = bf16[512,1024]{1,0:T(8,128)(2,1)} fusion(f32[512,1024]{1,0:T(8,128)} %get-tuple-element.8, bf16[2048,1024]{1,0:T(8,128)(2,1)} %all-gather.5.cloned.1.call-done, bf16[64,8,16,128]{3,2,1,0:T(8,128)(2,1)} %bitcast.29, f32[512]{0:T(512)S(1)} %multiply_bitcast_fusion), kind=kOutput, calls=%fused_computation.8 | convolution fusion | flops 2149580800 | bytes 9439232 | tf_op jit(solution)/shard_map/dot_general | solution.py:26
  (6 shorter events, 0.0 us)
Async XLA Ops:
  6.5 59.6 %copy-start = (bf16[4,16,128,128]{3,2,1,0:T(8,128)(2,1)S(1)}, bf16[4,16,128,128]{3,2,1,0:T(8,128)(2,1)}, u32[]{:S(2)}) copy-start(bf16[4,16,128,128]{3,2,1,0:T(8,128)(2,1)} %param.9) | copy-start | bytes 6291460
  15.5 21.1 %all-to-all-start = ((s32[128,4,1]{1,2,0:T(1,128)}), s32[128,4,1]{1,2,0:T(1,128)S(1)}, u32[]{:S(2)}, u32[]{:S(2)}) async-start(s32[128,4,1]{1,2,0:T(1,128)} %bitcast), calls=%async_computation | async-start | bytes 131072 | tf_op jit(solution)/shard_map/all_to_all | solution.py:48
  36.6 24.4 %all-to-all-start.1 = ((bf16[128,4,1024]{2,1,0:T(4,128)(2,1)}), bf16[128,4,1024]{2,1,0:T(4,128)(2,1)S(1)}, u32[]{:S(2)}, u32[]{:S(2)}) async-start(bf16[128,4,1024]{2,1,0:T(4,128)(2,1)} %all_to_all.16), calls=%async_computation.1 | async-start | bytes 2097152 | tf_op jit(solution)/shard_map/all_to_all | solution.py:45
  41.6 68.6 %all-gather.3.cloned.1.call-start = ((), (), s32[]{:S(2)}) async-start(), calls=%async_computation.2 | async-start | bytes 5242880 | tf_op jit(solution)/shard_map/all_gather | solution.py:56
  62.1 4.0 %copy-start.2 = (s32[4]{0:T(128)S(1)}, s32[4]{0:T(128)}, u32[]{:S(2)}) copy-start(s32[4]{0:T(128)} %param.8) | copy-start | bytes 52
  62.1 4.0 %copy-start.1 = (s32[4,16]{1,0:T(4,128)S(1)}, s32[4,16]{1,0:T(4,128)}, u32[]{:S(2)}) copy-start(s32[4,16]{1,0:T(4,128)} %param.7) | copy-start | bytes 772
  65.8 100.0 %all-gather.5.cloned.1.call-start = ((), (), s32[]{:S(2)}) async-start(), calls=%async_computation.3 | async-start | bytes 5242880 | tf_op jit(solution)/shard_map/all_gather | solution.py:56
Sparse Core Ops, SparseCore 0:
  65.9 44.2 all-gather.2
  117.2 48.6 all-gather.4
where the time goes:
time: 180 us; the launch traced here: 179 us
  waiting for transfers between devices  112 us (62%)
  matrix products  24.5 us (14%)
  starting transfers between devices  16.8 us (9%)
  between operations  13.5 us (8%)
  local copies, waits for them, and re-layouts  7.3 us (4%)
  other arithmetic  5.51 us (3%)
    all_gather x2, waiting for transfers between devices, group_panel(): return lax.all_gather(hidden, 'grp', axis=0, tiled=True)  89.3 us
    all_to_all x1, waiting for transfers between devices, shards(): lax.all_to_all(outgoing.astype(jnp.bfloat16), ('dom', 'grp'), split_axis=...  17.9 us
    dot_general x2, matrix products, propagate(): running = jnp.dot(dense, panel_rows, preferred_element_type=jnp.float32)  13.6 us
    all_to_all x1, starting transfers between devices, shards(): lax.all_to_all(places, ('dom', 'grp'), split_axis=0, concat_axis=0, tiled...  11.5 us
    all_to_all x1, starting transfers between devices, shards(): lax.all_to_all(outgoing.astype(jnp.bfloat16), ('dom', 'grp'), split_axis=...  4.99 us
    all_to_all x1, waiting for transfers between devices, shards(): lax.all_to_all(places, ('dom', 'grp'), split_axis=0, concat_axis=0, tiled...  4.77 us
    sort x1, other arithmetic, shards(): send_order = jnp.argsort(target_dev, stable=True)  3.77 us
    dot_general x1, matrix products, shards(): jnp.dot(place_pick, arrived, precision=lax.Precision.HIGHEST, preferred_e...  3.69 us
  transfers between devices with their start and end apart: 4, of which 4 were waited for; matrix products, arithmetic and copies ran while one was open for 5% of the time, Pallas kernels for 0%

commit v1 on v0

--- a/solution.py
+++ b/solution.py
@@ -5,6 +5,13 @@
 
 STEPS = 2
 mix_weight = 0.3
+
+
+def swapped_in(array, mesh_axis, dim):
+    devices = lax.axis_size(mesh_axis)
+    blocks = jnp.stack([array for _ in range(devices)])
+    blocks = lax.all_to_all(blocks, mesh_axis, split_axis=0, concat_axis=0)
+    return jnp.concatenate(blocks, axis=dim)
 
 
 def propagate(base_rows, weight_table, list_table, count_table, panel_blocks, gather_panel):
@@ -53,7 +60,7 @@
     )
 
     def group_panel(hidden):
-        return lax.all_gather(hidden, "grp", axis=0, tiled=True)
+        return swapped_in(hidden, "grp", 0)
 
     panel_blocks = block_count * lax.axis_size("grp")
     return propagate(base_rows, edge_weights, nbr_blocks, nbr_count, panel_blocks, group_panel)

time: 180 us -> 176 us (0.978)
  blocking collectives: 0 us -> 50.1 us
  waiting for transfers between devices: 112 us -> 67.6 us
  between operations: 13.5 us -> 0.1 us
  matrix products: 24.5 us -> 19.7 us
  starting transfers between devices: 16.8 us -> 21.4 us
  local copies, waits for them, and re-layouts: 7.3 us -> 10.5 us
    all_gather x2 -> x0, waiting for transfers between devices: 89.3 us -> none  [group_panel(): return lax.all_gather(hidden, 'grp', axis=0, tiled=True)]
    all_to_all x0 -> x1, blocking collectives: none -> 50.1 us  [swapped_in(): blocks = lax.all_to_all(blocks, mesh_axis, split_axis=0, concat_axis=0)]
    all_to_all x0 -> x1, waiting for transfers between devices: none -> 44.9 us  [swapped_in(): blocks = lax.all_to_all(blocks, mesh_axis, split_axis=0, concat_axis=0)]
    all_to_all x0 -> x1, starting transfers between devices: none -> 4.99 us  [swapped_in(): blocks = lax.all_to_all(blocks, mesh_axis, split_axis=0, concat_axis=0)]
    dot_general x2, matrix products: 13.6 us -> 9.19 us  [propagate(): running = jnp.dot(dense, panel_rows, preferred_element_type=jnp.float32)]
    another operation x0 -> x2, local copies, waits for them, and re-layouts: none -> 3.13 us  [swapped_in(): blocks = jnp.stack([array for _ in range(devices)])]
  transfers between devices with their start and end apart: 4 -> 3, of which waited for: 4 -> 3; matrix products, arithmetic and copies ran while one was open for 5% -> 5% of each run, Pallas kernels for 0% -> 0%
where the time goes in v1:
time: 176 us; the launch traced here: 175 us
  waiting for transfers between devices  67.6 us (38%)
  blocking collectives  50.1 us (28%)
  starting transfers between devices  21.4 us (12%)
  matrix products  19.7 us (11%)
  local copies, waits for them, and re-layouts  10.5 us (6%)
  other arithmetic  5.57 us (3%)
    all_to_all x1, blocking collectives, swapped_in(): blocks = lax.all_to_all(blocks, mesh_axis, split_axis=0, concat_axis=0)  50.1 us
    all_to_all x1, waiting for transfers between devices, swapped_in(): blocks = lax.all_to_all(blocks, mesh_axis, split_axis=0, concat_axis=0)  44.9 us
    all_to_all x1, waiting for transfers between devices, shards(): lax.all_to_all(outgoing.astype(jnp.bfloat16), ('dom', 'grp'), split_axis=...  17.8 us
    all_to_all x1, starting transfers between devices, shards(): lax.all_to_all(places, ('dom', 'grp'), split_axis=0, concat_axis=0, tiled...  11.5 us
    dot_general x2, matrix products, propagate(): running = jnp.dot(dense, panel_rows, preferred_element_type=jnp.float32)  9.19 us
    all_to_all x1, starting transfers between devices, swapped_in(): blocks = lax.all_to_all(blocks, mesh_axis, split_axis=0, concat_axis=0)  4.99 us
    all_to_all x1, starting transfers between devices, shards(): lax.all_to_all(outgoing.astype(jnp.bfloat16), ('dom', 'grp'), split_axis=...  4.93 us
    all_to_all x1, waiting for transfers between devices, shards(): lax.all_to_all(places, ('dom', 'grp'), split_axis=0, concat_axis=0, tiled...  4.84 us
  transfers between devices with their start and end apart: 3, of which 3 were waited for; matrix products, arithmetic and copies ran while one was open for 5% of the time, Pallas kernels for 0%

profile of v1, /device:TPU:1, one launch (start us, length us, event | category | flops | bytes accessed | tf_op | source)
XLA Modules:
  0.0 175.0 jit_solution(3496477674563621151)
XLA Ops:
  0.0 0.0 copy-start
  0.0 0.8 add_select_fusion.1
  0.8 3.8 %sort.17 = (s32[512]{0:T(512)}, s32[512]{0:T(512)S(1)}) sort(s32[512]{0:T(512)S(1)} %add_select_fusion.1, s32[512]{0:T(512)S(1)} %iota.22), dimensions={0}, to_apply=%region_0.1 | sort | flops 4608 | bytes 8192 | tf_op jit(solution)/shard_map/jit(argsort)/sort | solution.py:44
  4.6 3.6 %gather_fusion = s32[512]{0:T(512)S(1)} fusion(s32[512]{0:T(512)} %param.6, s32[1024]{0:T(1024)S(1)} %pad_clamp_fusion), kind=kCustom, calls=%fused_computation | custom fusion | bytes 6144 | tf_op jit(solution)/shard_map/jit(_take)/gather | solution.py:50
  8.3 0.7 select_n.37
  9.0 11.5 %all-to-all-start = ((s32[128,4,1]{1,2,0:T(1,128)}), s32[128,4,1]{1,2,0:T(1,128)S(1)}, u32[]{:S(2)}, u32[]{:S(2)}) async-start(s32[128,4,1]{1,2,0:T(1,128)} %bitcast), calls=%async_computation | async-start | bytes 131072 | tf_op jit(solution)/shard_map/all_to_all | solution.py:55
  20.5 3.6 %convolution_convert_fusion = bf16[512,1024]{1,0:T(8,128)(2,1)S(1)} fusion(f32[512,1024]{1,0:T(8,128)} %param.5, s32[512]{0:T(512)S(1)} %get-tuple-element.6), kind=kOutput, calls=%fused_computation.13 | convolution fusion | flops 3222011904 | bytes 3147776 | tf_op jit(solution)/shard_map/dot_general | solution.py:47
  24.1 1.2 all_to_all.22
  25.3 4.8 %all-to-all-done = s32[128,4,1]{1,2,0:T(1,128)S(1)} async-done(((s32[128,4,1]{1,2,0:T(1,128)}), s32[128,4,1]{1,2,0:T(1,128)S(1)}, u32[]{:S(2)}, u32[]{:S(2)}) %all-to-all-start) | async-done | bytes 2080 | tf_op jit(solution)/shard_map/all_to_all | solution.py:55
  30.1 4.9 %all-to-all-start.1 = ((bf16[128,4,1024]{2,1,0:T(4,128)(2,1)}), bf16[128,4,1024]{2,1,0:T(4,128)(2,1)S(1)}, u32[]{:S(2)}, u32[]{:S(2)}) async-start(bf16[128,4,1024]{2,1,0:T(4,128)(2,1)} %all_to_all.22), calls=%async_computation.1 | async-start | bytes 2097152 | tf_op jit(solution)/shard_map/all_to_all | solution.py:52
  35.1 0.6 broadcast.88
  35.7 0.8 reduce.4
  36.5 0.1 all_to_all.21
  36.6 17.8 %all-to-all-done.1 = bf16[128,4,1024]{2,1,0:T(4,128)(2,1)S(1)} async-done(((bf16[128,4,1024]{2,1,0:T(4,128)(2,1)}), bf16[128,4,1024]{2,1,0:T(4,128)(2,1)S(1)}, u32[]{:S(2)}, u32[]{:S(2)}) %all-to-all-start.1) | async-done | bytes 1048608 | tf_op jit(solution)/shard_map/all_to_all | solution.py:52
  54.5 1.1 all_to_all.24
  55.6 3.3 %fusion.26 = (bf16[512,1024]{1,0:T(8,128)(2,1)S(1)}, f32[512,1024]{1,0:T(8,128)}) fusion(bf16[512,1024]{1,0:T(8,128)(2,1)} %all_to_all.24, s32[512]{0:T(512)S(1)} %add_select_fusion), kind=kOutput, calls=%fused_computation.40 | convolution fusion | flops 537657344 | bytes 4196352 | tf_op jit(solution)/shard_map/dot_general | solution.py:58
  58.9 2.6 %stack.4 = bf16[4,512,1024]{2,1,0:T(8,128)(2,1)} broadcast(bf16[512,1024]{1,0:T(8,128)(2,1)S(1)} %get-tuple-element.7), dimensions={1,2} | broadcast | bytes 5242880 | tf_op jit(solution)/shard_map/stack | solution.py:12
  61.5 0.0 copy-start.4
  61.5 0.0 copy-start.3
  61.5 5.0 %all-to-all-start.2 = ((bf16[4,512,1024]{2,1,0:T(8,128)(2,1)}), bf16[4,512,1024]{2,1,0:T(8,128)(2,1)}, u32[]{:S(2)}, u32[]{:S(2)}) async-start(bf16[4,512,1024]{2,1,0:T(8,128)(2,1)} %stack.4), calls=%async_computation.2 | async-start | bytes 8388608 | tf_op jit(solution)/shard_map/all_to_all | solution.py:13
  66.5 0.0 copy-done.4
  66.5 0.1 iota_compare_fusion.5
  66.6 0.0 copy-done
  66.6 0.0 copy-done.3
  66.6 3.6 %convert_reduce_fusion = (f32[4,128]{1,0:T(4,128)S(1)}, bf16[4,16,128,128]{3,1,2,0:T(8,128)(2,1)}) fusion(bf16[4,16,128,128]{3,2,1,0:T(8,128)(2,1)S(1)} %copy-done, s32[4,16]{1,0:T(4,128)S(1)} %copy-done.3, pred[4,16]{1,0:T(4,128)(4,1)S(1)} %iota_compare_fusion.5), kind=kOutput, calls=%fused_computation.1 | convolution fusion | flops 36701696 | bytes 4196672 | tf_op jit(solution)/shard_map/bkg,bkpq->bpgq/dot_general | solution.py:24
  70.2 44.9 %all-to-all-done.2 = bf16[4,512,1024]{2,1,0:T(8,128)(2,1)} async-done(((bf16[4,512,1024]{2,1,0:T(8,128)(2,1)}), bf16[4,512,1024]{2,1,0:T(8,128)(2,1)}, u32[]{:S(2)}, u32[]{:S(2)}) %all-to-all-start.2) | async-done | bytes 4194336 | tf_op jit(solution)/shard_map/all_to_all | solution.py:13
  115.1 5.8 %add_convert_fusion.1 = bf16[512,1024]{1,0:T(8,128)(2,1)S(1)} fusion(f32[512,1024]{1,0:T(8,128)} %get-tuple-element.8, bf16[2048,1024]{1,0:T(8,128)(2,1)} %bitcast.4, bf16[64,8,16,128]{3,2,1,0:T(8,128)(2,1)} %bitcast.31, f32[512]{0:T(512)S(1)} %multiply_bitcast_fusion), kind=kOutput, calls=%fused_computation.9 | convolution fusion | flops 2149580800 | bytes 9439232 | tf_op jit(solution)/shard_map/dot_general | solution.py:33
  120.9 0.5 stack.5
  121.4 0.0 copy-start.1
  121.5 0.0 copy-start.2
  121.5 50.1 %all_to_all.31 = bf16[4,512,1024]{2,1,0:T(8,128)(2,1)S(1)} all-to-all(bf16[4,512,1024]{2,1,0:T(8,128)(2,1)S(1)} %stack.5), channel_id=1, replica_groups=mesh['dom'=32,'grp'=4] {'grp'}, dimensions={0} | all-to-all | bytes 8388608 | tf_op jit(solution)/shard_map/all_to_all | solution.py:13
  171.6 0.0 copy-done.1
  171.6 0.0 copy-done.2
  171.6 3.4 %add_convert_fusion = bf16[512,1024]{1,0:T(8,128)(2,1)} fusion(f32[512,1024]{1,0:T(8,128)S(1)} %copy-done.2, bf16[2048,1024]{1,0:T(8,128)(2,1)S(1)} %bitcast.30, bf16[64,8,16,128]{3,2,1,0:T(8,128)(2,1)S(1)} %bitcast.32, f32[512]{0:T(512)S(1)} %multiply_bitcast_fusion), kind=kOutput, calls=%fused_computation.8 | convolution fusion | flops 2149580800 | bytes 9439232 | tf_op jit(solution)/shard_map/dot_general | solution.py:33
  (6 shorter events, 0.0 us)
Async XLA Ops:
  0.0 66.6 %copy-start = (bf16[4,16,128,128]{3,2,1,0:T(8,128)(2,1)S(1)}, bf16[4,16,128,128]{3,2,1,0:T(8,128)(2,1)}, u32[]{:S(2)}) copy-start(bf16[4,16,128,128]{3,2,1,0:T(8,128)(2,1)} %param.9) | copy-start | bytes 6291460
  9.0 21.1 %all-to-all-start = ((s32[128,4,1]{1,2,0:T(1,128)}), s32[128,4,1]{1,2,0:T(1,128)S(1)}, u32[]{:S(2)}, u32[]{:S(2)}) async-start(s32[128,4,1]{1,2,0:T(1,128)} %bitcast), calls=%async_computation | async-start | bytes 131072 | tf_op jit(solution)/shard_map/all_to_all | solution.py:55
  30.1 24.4 %all-to-all-start.1 = ((bf16[128,4,1024]{2,1,0:T(4,128)(2,1)}), bf16[128,4,1024]{2,1,0:T(4,128)(2,1)S(1)}, u32[]{:S(2)}, u32[]{:S(2)}) async-start(bf16[128,4,1024]{2,1,0:T(4,128)(2,1)} %all_to_all.22), calls=%async_computation.1 | async-start | bytes 2097152 | tf_op jit(solution)/shard_map/all_to_all | solution.py:52
  61.5 5.0 %copy-start.4 = (s32[4]{0:T(128)S(1)}, s32[4]{0:T(128)}, u32[]{:S(2)}) copy-start(s32[4]{0:T(128)} %param.8) | copy-start | bytes 52
  61.5 5.1 %copy-start.3 = (s32[4,16]{1,0:T(4,128)S(1)}, s32[4,16]{1,0:T(4,128)}, u32[]{:S(2)}) copy-start(s32[4,16]{1,0:T(4,128)} %param.7) | copy-start | bytes 772
  61.5 53.6 %all-to-all-start.2 = ((bf16[4,512,1024]{2,1,0:T(8,128)(2,1)}), bf16[4,512,1024]{2,1,0:T(8,128)(2,1)}, u32[]{:S(2)}, u32[]{:S(2)}) async-start(bf16[4,512,1024]{2,1,0:T(8,128)(2,1)} %stack.4), calls=%async_computation.2 | async-start | bytes 8388608 | tf_op jit(solution)/shard_map/all_to_all | solution.py:13
  121.4 50.2 %copy-start.1 = (bf16[4,16,128,128]{3,1,2,0:T(8,128)(2,1)S(1)}, bf16[4,16,128,128]{3,1,2,0:T(8,128)(2,1)}, u32[]{:S(2)}) copy-start(bf16[4,16,128,128]{3,1,2,0:T(8,128)(2,1)} %get-tuple-element.10) | copy-start | bytes 6291460
  121.5 50.1 %copy-start.2 = (f32[512,1024]{1,0:T(8,128)S(1)}, f32[512,1024]{1,0:T(8,128)}, u32[]{:S(2)}) copy-start(f32[512,1024]{1,0:T(8,128)} %get-tuple-element.8) | copy-start | bytes 6291460
